TPU v7x, 512 devices: a whole 4x4x16 slice. The times are simulated.
512 devices in a mesh: rep: 2 (over core), vocab: 64 (over z, x), tok: 4 (over y).
Axes of the slice: x: 4, y: 4, z: 16, core: 2. Of those that a mesh axis runs over, the one named last changes fastest.
Arguments:
- hidden: bfloat16 [2, 384, 3072], P('rep', None, 'tok'), may hold values from -48 to 48
- head_weight: bfloat16 [2, 3072, 81920], P('rep', 'tok', 'vocab'), may hold values from -0.5 to 0.5
- token_ids: int32 [384], replicated, may hold values from 0 to 81919
Outputs:
- per_token_loss: float32 [2, 384], P('rep', 'tok')
- weight_grad: bfloat16 [2, 3072, 81920], P('rep', 'tok', 'vocab')
- hidden_grad: bfloat16 [2, 384, 3072], P('rep', 'vocab', 'tok')
All inputs are finite; a program needn't handle non-finite values.
Results may differ from a plain program's by a relative error of at most 0.0041.
Values may be sent and summed in bfloat16 or wider, within the bound.
A program may use at most 64 MiB of HBM per device.

v0:
```python
import jax
import jax.numpy as jnp
from jax import lax
from jax.sharding import PartitionSpec as P

smoothing_divisor = 2.0
mimicry_coefficient = 0.5


def from_partner(array, axis, distance):
    return lax.ppermute(array, axis, [(i, i ^ 1 << distance) for i in range(lax.axis_size(axis))])


def row_statistics(score_matrix, target_hit):
    picked_local = jnp.sum(jnp.where(target_hit, score_matrix, 0.0), axis=1)
    largest_entry_each = lax.pmax(jnp.max(score_matrix, axis=1), "vocab")
    centered_scores = score_matrix - largest_entry_each[:, None]
    norm_sum, smoothed_accumulated, chosen_target_score = lax.psum(
        (
            jnp.sum(jnp.exp(centered_scores), axis=1),
            jnp.sum(jnp.exp(centered_scores / smoothing_divisor), axis=1),
            picked_local,
        ),
        "vocab",
    )
    return (largest_entry_each, norm_sum, smoothed_accumulated, chosen_target_score)


def body(hidden, head_weight, token_ids):
    features = hidden[0]
    weight = head_weight[0]
    total_tokens = features.shape[0]
    vocab_shard = weight.shape[1]
    owned_tokens = total_tokens // lax.axis_size("tok")
    token_first = lax.axis_index("tok") * owned_tokens
    score_matrix = lax.psum(jnp.dot(features, weight, preferred_element_type=jnp.float32), "tok")
    columns = lax.axis_index("vocab") * vocab_shard + lax.broadcasted_iota(
        jnp.int32, score_matrix.shape, 1
    )
    target_hit = columns == token_ids[:, None]
    largest_entry_each, norm_sum, smoothed_accumulated, chosen_target_score = row_statistics(
        score_matrix, target_hit
    )
    normalizer_logarithm = largest_entry_each + jnp.log(norm_sum)
    smoothed_logarithm = (
        score_matrix / smoothing_divisor
        - (largest_entry_each / smoothing_divisor + jnp.log(smoothed_accumulated))[:, None]
    )
    teacher_log = from_partner(smoothed_logarithm, "rep", 0)
    guide_distribution = jnp.exp(teacher_log)
    spread_part = jnp.sum(guide_distribution * (teacher_log - smoothed_logarithm), axis=1)
    score_grad = (
        jnp.exp(score_matrix - normalizer_logarithm[:, None])
        - target_hit.astype(jnp.float32)
        + mimicry_coefficient
        * smoothing_divisor
        * (jnp.exp(smoothed_logarithm) - guide_distribution)
    ).astype(jnp.bfloat16)
    weight_grad = lax.dot_general(
        features, score_grad, (((0,), (0,)), ((), ())), preferred_element_type=jnp.float32
    ).astype(jnp.bfloat16)
    vocab_rows = total_tokens // lax.axis_size("vocab")
    vocab_first = lax.axis_index("vocab") * vocab_rows
    hidden_whole, relative_entropy_amount = lax.psum(
        (
            lax.dot_general(
                score_grad, weight, (((1,), (1,)), ((), ())), preferred_element_type=jnp.float32
            ),
            spread_part,
        ),
        "vocab",
    )
    hidden_part = lax.dynamic_slice_in_dim(hidden_whole, vocab_first, vocab_rows, 0)
    per_token_loss = (
        normalizer_logarithm
        - chosen_target_score
        + mimicry_coefficient * smoothing_divisor * smoothing_divisor * relative_entropy_amount
    )
    per_token_loss = lax.dynamic_slice_in_dim(per_token_loss, token_first, owned_tokens, 0)
    return (per_token_loss[None], weight_grad[None], hidden_part.astype(jnp.bfloat16)[None])


def solution(mesh):
    return jax.shard_map(
        body,
        mesh=mesh,
        in_specs=(P("rep", None, "tok"), P("rep", "tok", "vocab"), P()),
        out_specs=(P("rep", "tok"), P("rep", "tok", "vocab"), P("rep", "vocab", "tok")),
        check_vma=False,
    )
```

profile of v0, /device:TPU:8, one launch (start us, length us, event | category | flops | bytes accessed | tf_op | source)
XLA Modules:
  0.0 691.4 jit_solution(14041247738519747853)
XLA Ops:
  7.2 0.0 copy-start
  7.2 0.0 all-reduce.5.cloned.1.call-start
  7.2 1.5 copy-done
  8.7 3.3 fusion.7
  12.0 0.0 all-reduce.5.cloned.1.call-update
  12.0 75.4 %all-reduce.5.cloned.1.call-done = f32[384,1280]{1,0:T(8,128)} async-done(((f32[384,1280]{1,0:T(8,128)}), f32[384,1280]{1,0:T(8,128)}) %all-reduce.5.cloned.1.call-update) | async-done | bytes 1966096 | tf_op jit(solution)/shard_map/psum | solution.py:36
  87.4 1.7 reduce_max.9
  89.1 144.2 %pmax.7 = f32[384]{0:T(512)S(1)} all-reduce(f32[384]{0:T(512)S(1)} %reduce_max.9), channel_id=1, replica_groups=mesh['rep'=2,'vocab'=64,'tok'=4] {'vocab'}, use_global_device_ids=true, to_apply=%region_2.3 | all-reduce | flops 384 | bytes 3072 | tf_op jit(solution)/shard_map/pmax | solution.py:16
  233.3 2.2 exponential_reduce_fusion.1
  235.5 138.0 %all-reduce.1 = (f32[384]{0:T(512)S(1)}, f32[384]{0:T(512)S(1)}) all-reduce(f32[384]{0:T(512)S(1)} %get-tuple-element.7, f32[384]{0:T(512)S(1)} %get-tuple-element.6), channel_id=1, replica_groups=mesh['rep'=2,'vocab'=64,'tok'=4] {'vocab'}, use_global_device_ids=true, to_apply=%region_8.9 | all-reduce | flops 768 | bytes 6144 | tf_op jit(solution)/shard_map/psum | solution.py:18
  373.5 0.0 copy-start.1
  373.5 3.0 multiply_subtract_fusion
  376.5 1.9 collective-permute-start
  378.4 4.3 collective-permute-done
  382.7 0.0 copy-done.1
  382.7 0.0 copy-start.2
  382.7 3.7 fusion.1
  386.4 0.0 copy-done.2
  386.4 2.5 fusion
  388.9 1.0 fusion.5
  389.9 4.0 copy.6
  393.9 288.8 %all-reduce.6 = (f32[384]{0:T(512)S(1)}, f32[384]{0:T(512)S(1)}, bf16[384,768]{1,0:T(8,128)(2,1)}) all-reduce(f32[384]{0:T(512)S(1)} %get-tuple-element.9, f32[384]{0:T(512)S(1)} %get-tuple-element.8, f32[384,768]{1,0:T(8,128)S(1)} %fusion.5), channel_id=1, replica_groups=mesh['rep'=2,'vocab'=64,'tok'=4] {'vocab'}, use_global_device_ids=true, to_apply=%region_10.11 | all-reduce | flops 295680 | bytes 1775616 | tf_op jit(solution)/shard_map/psum | solution.py:64
  682.6 1.3 fusion.11
  684.0 0.6 dynamic-slice_bitcast_fusion
  (3 shorter events, 0.0 us)
Async XLA Ops:
  7.2 1.6 copy-start
  7.2 80.2 %all-reduce.5.cloned.1.call-start = ((), (), s32[]{:S(2)}) async-start(), calls=%async_computation | async-start | bytes 3932160 | tf_op jit(solution)/shard_map/psum | solution.py:36
  373.5 9.2 %copy-start.1 = (s32[384]{0:T(512)S(1)}, s32[384]{0:T(512)}, u32[]{:S(2)}) copy-start(s32[384]{0:T(512)} %param.5) | copy-start | bytes 4612
  376.5 6.2 collective-permute-start
  382.7 3.7 copy-start.2
Sparse Core Ops, SparseCore 0:
  12.1 75.2 all-reduce.4
where the time goes:
time: 692 us; the launch traced here: 691 us
  blocking collectives  571 us (83%)
  waiting for transfers between devices  79.6 us (12%)
  between operations  14.1 us (2%)
  other arithmetic  10.7 us (2%)
  local copies, waits for them, and re-layouts  7.41 us (1%)
    psum x1, blocking collectives, body(): lax.psum((lax.dot_general(score_grad, weight, (((1,), (1,)), ((), ())), p...  289 us
    pmax x1, blocking collectives, row_statistics(): largest_entry_each = lax.pmax(jnp.max(score_matrix, axis=1), 'vocab')  144 us
    psum x1, blocking collectives, row_statistics(): lax.psum((jnp.sum(jnp.exp(centered_scores), axis=1), jnp.sum(jnp.exp(cent...  138 us
    psum x1, waiting for transfers between devices, body(): lax.psum(jnp.dot(features, weight, preferred_element_type=jnp.float32), '...  75.4 us
  transfers between devices with their start and end apart: 2, of which 2 were waited for; matrix products, arithmetic and copies ran while one was open for 0% of the time, Pallas kernels for 0%

commit v1 on v0

v1 whole, which is shorter than its diff:
```python
import functools

import jax
import jax.numpy as jnp
from jax import lax
from jax.experimental import pallas as pl
from jax.experimental.pallas import tpu as pltpu
from jax.sharding import PartitionSpec as P

F32, BF16 = jnp.float32, jnp.bfloat16
NX, NZ, NY = 4, 16, 4
CHUNKS = 8
ROWS = 48
HALF = 640
MESH = pl.DeviceIdType.MESH


def rows_of(m):
    return pl.ds(pl.multiple_of(m * ROWS, 16), ROWS)


def dot(a, b, ca, cb):
    return lax.dot_general(a, b, (((ca,), (cb,)), ((), ())), preferred_element_type=F32)


def kernel(
    hid, wt, ids, loss_out, wg_out, hg_out,
    w_v, h_v, ht_v, acc, fbuf, cbuf, rx, pr, lg, sg, s1, hgs, xr, zs, zr, wg_v, xst, zst, lb,
    load_sem, out_sem, a_send, a_recv, st_send, st_recv, zst_send, zst_recv, l_send, l_recv,
    g_send, g_recv, x_send, x_recv, z_send, z_recv,
):
    c = lax.axis_index("rep")
    v = lax.axis_index("vocab")
    y = lax.axis_index("tok")
    z, x = v // NX, v % NX
    pc = 1 - c
    R, L, O = (y + 1) % NY, (y + 3) % NY, (y + 2) % NY
    mine = y + 4 * c
    cores = (c, pc)

    def xid(d):
        return {"vocab": z * NX + (x + d) % NX}

    def zid(zz):
        return {"vocab": zz * NX + x}

    def yid(core, yy):
        return {"rep": core, "tok": yy}

    loads = [
        pltpu.make_async_copy(hid.at[0], h_v, load_sem.at[0]),
        pltpu.make_async_copy(wt.at[0, :, pl.ds(0, HALF)], w_v.at[0], load_sem.at[1]),
        pltpu.make_async_copy(wt.at[0, :, pl.ds(HALF, HALF)], w_v.at[1], load_sem.at[2]),
    ]
    for cp in loads:
        cp.start()

    barrier = pltpu.get_barrier_semaphore()
    peers = [yid(cores[s], yy) for s in range(2) for yy in (y, R, L, O)][1:]
    peers += [xid(d) for d in range(1, NX)] + [zid((z + d) % NZ) for d in range(1, NZ)]
    for p in peers:
        pl.semaphore_signal(barrier, inc=1, device_id=p, device_id_type=MESH)

    def remote(src, dst, ss, rs, dev):
        return pltpu.make_async_remote_copy(
            src_ref=src, dst_ref=dst, send_sem=ss, recv_sem=rs, device_id=dev, device_id_type=MESH
        )

    sends = []

    def start(cp):
        cp.start()
        sends.append(cp)

    loads[0].wait()
    for a in range(2):
        loads[1 + a].wait()
        part = dot(h_v[...], w_v[a], 1, 0)
        acc[a] = part
        if a == 0:
            pl.semaphore_wait(barrier, len(peers))
        near, far = ((R, L), (L, R))[a]
        for s in range(2):
            i = 2 * a + s
            start(remote(acc.at[a, rows_of(O + 4 * cores[s])], fbuf.at[a, s],
                         a_send.at[i], a_recv.at[i], yid(c, near)))
        for s in range(2):
            i = 4 + 2 * a + s
            start(remote(acc.at[a, rows_of(far + 4 * cores[s])], rx.at[0, a, s],
                         a_send.at[i], a_recv.at[i], yid(cores[s], far)))
        start(remote(acc.at[a, rows_of(y + 4 * pc)], pr.at[a],
                     a_send.at[12 + a], a_recv.at[12 + a], yid(pc, y)))
    for s in range(2):
        for a in range(2):
            i = 2 * a + s
            near = (R, L)[a]
            m = rows_of(near + 4 * cores[s])
            remote(acc.at[a, m], fbuf.at[a, s], a_send.at[i], a_recv.at[i], yid(c, near)).wait_recv()
            cbuf[a, s] = acc[a, m] + fbuf[a, s]
            start(remote(cbuf.at[a, s], rx.at[1, a, s], a_send.at[8 + i], a_recv.at[8 + i],
                         yid(cores[s], near)))

    ht_v[...] = h_v[...].T
    spot = lax.broadcasted_iota(jnp.int32, (ROWS, 384), 1) - lax.broadcasted_iota(jnp.int32, (ROWS, 384), 0)
    id_col = jnp.sum(jnp.where(spot == mine * ROWS, ids[...], 0), axis=1, keepdims=True) - v * (2 * HALF)

    for a in range(2):
        remote(acc.at[a, rows_of(mine)], pr.at[a], a_send.at[12 + a], a_recv.at[12 + a], yid(pc, y)).wait_recv()
    for s in range(2):
        for a in range(2):
            for k in range(2):
                i = 4 + 4 * k + 2 * a + s
                remote(cbuf.at[a, s], rx.at[k, a, s], a_send.at[i], a_recv.at[i], yid(c, R)).wait_recv()
            own = acc[a, rows_of(mine)] if s == 0 else pr[a]
            lg[s, a] = own + rx[0, a, s] + rx[1, a, s]

    cols = lax.broadcasted_iota(jnp.int32, (ROWS, HALF), 1)
    lane = lax.broadcasted_iota(jnp.int32, (ROWS, 128), 1)
    tiles = []
    pad = jnp.zeros((16, 128), F32)
    for s in range(2):
        la, lbh = lg[s, 0], lg[s, 1]
        top = jnp.maximum(jnp.max(la, axis=1, keepdims=True), jnp.max(lbh, axis=1, keepdims=True))
        tot = [0.0] * 4
        for a, l in ((0, la), (1, lbh)):
            e = jnp.exp((l - top) * 0.5)
            hit = cols == id_col - a * HALF
            for n, term in enumerate((e * e, e, jnp.where(hit, l, 0.0), e * (0.5 * (l - lg[1 - s, a])))):
                tot[n] = tot[n] + jnp.sum(term, axis=1, keepdims=True)
        tile = jnp.where(lane == 0, top, 0.0)
        for n in range(4):
            tile = jnp.where(lane == n + 1, tot[n], tile)
        tiles += [tile, pad]
    stat = jnp.concatenate(tiles, axis=0).T[:8]

    def merge(parts):
        tops = functools.reduce(jnp.maximum, [p[0:1] for p in parts])
        total = [0.0] * 4
        for p in parts:
            f = jnp.exp((p[0:1] - tops) * 0.5)
            for n, w in enumerate((f * f, f, 1.0, f)):
                total[n] = total[n] + p[n + 1:n + 2] * w
        return tops, total

    xst[0] = stat
    for d in range(1, NX):
        start(remote(xst.at[0], xst.at[d], st_send.at[d], st_recv.at[d], xid(d)))
    for d in range(1, NX):
        remote(xst.at[0], xst.at[d], st_send.at[d], st_recv.at[d], xid(d)).wait_recv()
    tops, total = merge([xst[d] for d in range(NX)])
    zst[0] = jnp.concatenate([tops] + total + [jnp.zeros((3, 128), F32)], axis=0)
    for d in range(1, NZ):
        start(remote(zst.at[0], zst.at[d], zst_send.at[d], zst_recv.at[d], zid((z + d) % NZ)))
    for d in range(1, NZ):
        remote(zst.at[0], zst.at[d], zst_send.at[d], zst_recv.at[d], zid((z + d) % NZ)).wait_recv()
    tops, total = merge([zst[d] for d in range(NZ)])
    log_total = tops + jnp.log(total[0])
    tau_total = tops * 0.5 + jnp.log(total[1])
    ratio = pltpu.roll(total[3] / total[1] - tau_total, 64, 1) + tau_total
    loss = log_total - total[2] + 2.0 * ratio
    back = jnp.concatenate([log_total, tau_total, jnp.zeros((126, 128), F32)], axis=0).T

    mr = rows_of(mine)
    for a in range(2):
        hit = jnp.where(cols == id_col - a * HALF, 1.0, 0.0)
        l = [lg[0, a], lg[1, a]]
        q = [jnp.exp(l[s] * 0.5 - back[64 * s:64 * s + ROWS, 1:2]) for s in range(2)]
        for s in range(2):
            g = (jnp.exp(l[s] - back[64 * s:64 * s + ROWS, 0:1]) - hit + (q[s] - q[1 - s])).astype(BF16)
            if s == 0:
                sg[a, mr] = g
            else:
                s1[a] = g
        for s in range(2):
            src = sg.at[a, mr] if s == 0 else s1.at[a]
            i = 2 * a + s
            start(remote(src, sg.at[a, mr], g_send.at[i], g_recv.at[i], yid(cores[s], (R, L)[a])))
        start(remote(s1.at[a], sg.at[a, mr], g_send.at[12 + a], g_recv.at[12 + a], yid(pc, y)))
    for a in range(2):
        for s in range(2):
            src = sg.at[a, mr] if s == 0 else s1.at[a]
            i = 4 + 2 * a + s
            start(remote(src, sg.at[a, mr], g_send.at[i], g_recv.at[i], yid(cores[s], (L, R)[a])))

    lb[mine] = jnp.concatenate([loss, jnp.zeros((7, 128), F32)], axis=0)
    for e in range(1, CHUNKS):
        t = (mine + e) % CHUNKS
        start(remote(lb.at[mine], lb.at[mine], l_send.at[e], l_recv.at[mine], yid(t // 4, t % 4)))

    rr = lax.broadcasted_iota(jnp.int32, (64, ROWS), 0)
    tt = lax.broadcasted_iota(jnp.int32, (64, ROWS), 1)
    inner = rr % 8
    place = jnp.where((tt == (rr % 16) // 8 * 24 + rr // 16 * 6 + inner) & (inner < 6), 1.0, 0.0).astype(BF16)

    def hidden_part(k, m):
        r = rows_of(m)
        part = dot(sg[0, r], w_v[0], 1, 1) + dot(sg[1, r], w_v[1], 1, 1)
        hgs[k] = dot(place, part.astype(BF16), 1, 0).astype(BF16)
        for d in range(1, NX):
            xx = pl.multiple_of((x + d) % NX * 16, 16)
            start(remote(hgs.at[k, pl.ds(xx, 16)], xr.at[k, d], x_send.at[k, d], x_recv.at[k, d], xid(d)))

    def x_sum(k, m):
        total = hgs[k, pl.ds(pl.multiple_of(x * 16, 16), 16)].astype(F32)
        for d in range(1, NX):
            remote(hgs.at[k, pl.ds(0, 16)], xr.at[k, d], x_send.at[k, d], x_recv.at[k, d], xid(d)).wait_recv()
            total = total + xr[k, d].astype(F32)
        for i in range(2):
            t = total[8 * i:8 * i + 8]
            zs[k, i] = jnp.concatenate([t[:, :384], t[:, 384:]], axis=0).astype(BF16)
            zz = 2 * m + i
            d = (zz - z + NZ) % NZ

            @pl.when(d != 0)
            def _():
                remote(zs.at[k, i], zr.at[d], z_send.at[d], z_recv.at[d], zid(zz)).start()

            @pl.when(d == 0)
            def _():
                zr[0] = zs[k, i]

    def got(i, a, m, dev):
        remote(sg.at[a, rows_of(m)], sg.at[a, rows_of(m)], g_send.at[i], g_recv.at[i], dev).wait_recv()

    order = [mine, y + 4 * pc] + [n + 4 * cores[s] for s in range(2) for n in (L, R)]
    order += [O + 4 * cores[s] for s in range(2)]
    hidden_part(0, order[0])
    for a in range(2):
        got(12 + a, a, order[1], yid(pc, y))
    hidden_part(1, order[1])
    x_sum(0, order[0])
    for s in range(2):
        for a in range(2):
            m = (L, R)[a] + 4 * cores[s]
            got(2 * a + s, a, m, yid(c, L))
            start(remote(sg.at[a, rows_of(m)], sg.at[a, rows_of(m)], g_send.at[8 + 2 * a + s],
                         g_recv.at[8 + 2 * a + s], yid(c, (R, L)[a])))
    k = 2
    for s in range(2):
        for a in range(2):
            m = order[k]
            got(4 + 2 * (1 - a) + s, 1 - a, m, yid(c, L))
            hidden_part(k, m)
            x_sum(k - 1, order[k - 1])
            k += 1
    for s in range(2):
        for a in range(2):
            got(8 + 2 * a + s, a, order[k], yid(c, L))
        hidden_part(k, order[k])
        x_sum(k - 1, order[k - 1])
        k += 1

    outs = []
    for a in range(2):
        wg_v[a] = dot(ht_v[...], sg[a], 1, 0).astype(BF16)
        cp = pltpu.make_async_copy(wg_v.at[a], wg_out.at[0, :, pl.ds(a * HALF, HALF)], out_sem.at[a])
        cp.start()
        outs.append(cp)
        if a == 0:
            x_sum(k - 1, order[k - 1])

    for e in range(1, CHUNKS):
        t = (mine + e) % CHUNKS
        remote(lb.at[t], lb.at[t], l_send.at[e], l_recv.at[t], yid(pc, y)).wait_recv()
    pieces = []
    for i in range(2):
        m = 2 * y + i
        row = lb[m][0:1]
        pieces.append(jnp.where(m // 4 == c, row, pltpu.roll(row, 64, 1)))
    lanes = lax.broadcasted_iota(jnp.int32, (1, 128), 1)
    loss_out[...] = jnp.where(lanes < ROWS, pieces[0], pltpu.roll(pieces[1], ROWS, 1))[:, :96]

    for d in range(1, NZ):
        remote(zr.at[d], zr.at[d], z_send.at[d], z_recv.at[d], zid(z)).wait_recv()
    total = zr[0].astype(F32)
    for d in range(1, NZ):
        total = total + zr[d].astype(F32)
    hg_out[0] = jnp.concatenate([total[:8], total[8:]], axis=1)[:6].astype(BF16)

    for cp in sends:
        cp.wait_send()
    for d in range(1, NZ):
        remote(zr.at[d], zr.at[d], z_send.at[d], z_recv.at[d], zid((z + d) % NZ)).wait_send()
    for cp in outs:
        cp.wait()


def body(hidden, head_weight, token_ids):
    dma = pltpu.SemaphoreType.DMA
    return pl.pallas_call(
        kernel,
        out_shape=(
            jax.ShapeDtypeStruct((1, 96), F32),
            jax.ShapeDtypeStruct((1, 768, 2 * HALF), BF16),
            jax.ShapeDtypeStruct((1, 6, 768), BF16),
        ),
        in_specs=[
            pl.BlockSpec(memory_space=pl.ANY),
            pl.BlockSpec(memory_space=pl.ANY),
            pl.BlockSpec(memory_space=pltpu.VMEM),
        ],
        out_specs=(
            pl.BlockSpec(memory_space=pltpu.VMEM),
            pl.BlockSpec(memory_space=pl.ANY),
            pl.BlockSpec(memory_space=pltpu.VMEM),
        ),
        scratch_shapes=[
            pltpu.VMEM((2, 768, HALF), BF16),
            pltpu.VMEM((384, 768), BF16),
            pltpu.VMEM((768, 384), BF16),
            pltpu.VMEM((2, 384, HALF), F32),
            pltpu.VMEM((2, 2, ROWS, HALF), F32),
            pltpu.VMEM((2, 2, ROWS, HALF), F32),
            pltpu.VMEM((2, 2, 2, ROWS, HALF), F32),
            pltpu.VMEM((2, ROWS, HALF), F32),
            pltpu.VMEM((2, 2, ROWS, HALF), F32),
            pltpu.VMEM((2, 384, HALF), BF16),
            pltpu.VMEM((2, ROWS, HALF), BF16),
            pltpu.VMEM((CHUNKS, 64, 768), BF16),
            pltpu.VMEM((CHUNKS, NX, 16, 768), BF16),
            pltpu.VMEM((CHUNKS, 2, 16, 384), BF16),
            pltpu.VMEM((NZ, 16, 384), BF16),
            pltpu.VMEM((2, 768, HALF), BF16),
            pltpu.VMEM((NX, 8, 128), F32),
            pltpu.VMEM((NZ, 8, 128), F32),
            pltpu.VMEM((CHUNKS, 8, 128), F32),
            dma((3,)), dma((2,)),
            dma((14,)), dma((14,)),
            dma((NX,)), dma((NX,)),
            dma((NZ,)), dma((NZ,)),
            dma((CHUNKS,)), dma((CHUNKS,)),
            dma((14,)), dma((14,)),
            dma((CHUNKS, NX)), dma((CHUNKS, NX)),
            dma((NZ,)), dma((NZ,)),
        ],
        compiler_params=pltpu.CompilerParams(
            collective_id=0, has_side_effects=True, vmem_limit_bytes=48 * 1024 * 1024
        ),
        cost_estimate=pl.CostEstimate(flops=2400000000, bytes_accessed=5000000, transcendentals=400000),
    )(hidden, head_weight, token_ids.reshape(1, 384))


def solution(mesh):
    return jax.shard_map(
        body,
        mesh=mesh,
        in_specs=(P("rep", None, "tok"), P("rep", "tok", "vocab"), P()),
        out_specs=(P("rep", "tok"), P("rep", "tok", "vocab"), P("rep", "vocab", "tok")),
        check_vma=False,
    )
```

time: 692 us -> 81.7 us (0.12)
  the two profiles are of different devices: /device:TPU:8 before, /device:TPU:16 now
where the time goes in v1:
time: 81.7 us; the launch traced here: 81.5 us
  Pallas kernels  75.1 us (92%)
  local copies, waits for them, and re-layouts  5.68 us (7%)
    pallas_call x1, Pallas kernels, body(): pl.pallas_call(kernel, out_shape=(jax.ShapeDtypeStruct((1, 96), F32), jax...  75.1 us
    unnamed x7, local copies, waits for them, and re-layouts  4.99 us

profile of v1, /device:TPU:16, one launch (start us, length us, event | category | flops | bytes accessed | tf_op | source)
XLA Modules:
  0.0 81.5 jit_solution(3545387625874661240)
XLA Ops:
  0.6 0.7 reshape.9.ids
  1.3 0.0 copy-start
  1.3 1.5 %copy-done = bf16[1,768,1280]{2,1,0:T(8,128)(2,1)S(1)} copy-done((bf16[1,768,1280]{2,1,0:T(8,128)(2,1)S(1)}, bf16[1,768,1280]{2,1,0:T(8,128)(2,1)}, u32[]{:S(2)}) %copy-start) | copy-done | bytes 1966104
  2.9 0.0 copy-start.1
  2.9 1.1 %copy-done.1 = bf16[1,384,768]{2,1,0:T(8,128)(2,1)S(1)} copy-done((bf16[1,384,768]{2,1,0:T(8,128)(2,1)S(1)}, bf16[1,384,768]{2,1,0:T(8,128)(2,1)}, u32[]{:S(2)}) %copy-start.1) | copy-done | bytes 589848
  3.9 75.1 %shard_map.58 = (f32[1,96]{1,0:T(1,128)S(1)}, bf16[1,768,1280]{2,1,0:T(8,128)(2,1)S(1)}, bf16[1,6,768]{2,1,0:T(8,128)(2,1)S(1)}) custom-call(bf16[1,384,768]{2,1,0:T(8,128)(2,1)S(1)} %copy-done.1, bf16[1,768,1280]{2,1,0:T(8,128)(2,1)S(1)} %copy-done, s32[1,384]{1,0:T(1,128)S(1)} %reshape.9.ids), custom_call_target="tpu_custom_call" | custom-call | flops 2400000000 | bytes 5000000 | tf_op jit(solution)/shard_map/pallas_call | solution.py:290
  79.1 0.5 copy.9
  79.6 1.3 %copy.10 = bf16[1,768,1280]{2,1,0:T(8,128)(2,1)} copy(bf16[1,768,1280]{2,1,0:T(8,128)(2,1)S(1)} %get-tuple-element.7) | data formatting | bytes 3932160
  80.9 0.6 copy.11
Async XLA Ops:
  1.3 1.5 %copy-start = (bf16[1,768,1280]{2,1,0:T(8,128)(2,1)S(1)}, bf16[1,768,1280]{2,1,0:T(8,128)(2,1)}, u32[]{:S(2)}) copy-start(bf16[1,768,1280]{2,1,0:T(8,128)(2,1)} %wt.1) | copy-start | bytes 5898244
  2.9 1.1 %copy-start.1 = (bf16[1,384,768]{2,1,0:T(8,128)(2,1)S(1)}, bf16[1,384,768]{2,1,0:T(8,128)(2,1)}, u32[]{:S(2)}) copy-start(bf16[1,384,768]{2,1,0:T(8,128)(2,1)} %hid.1) | copy-start | bytes 1769476

commit v2 on v1

v2 whole, which is shorter than its diff:
```python
import functools

import jax
import jax.numpy as jnp
from jax import lax
from jax.experimental import pallas as pl
from jax.experimental.pallas import tpu as pltpu
from jax.sharding import PartitionSpec as P

F32, BF16, I16, I32 = jnp.float32, jnp.bfloat16, jnp.int16, jnp.int32
NX, NZ, NY = 4, 16, 4
CHUNKS = 8
ROWS = 48
HALF = 640
STEPS = 4
MESH = pl.DeviceIdType.MESH


def rows_of(m):
    return pl.ds(pl.multiple_of(m * ROWS, 16), ROWS)


def dot(a, b, ca, cb):
    return lax.dot_general(a, b, (((ca,), (cb,)), ((), ())), preferred_element_type=F32)


def iota(shape, dim):
    return lax.broadcasted_iota(I32, shape, dim)


def by24(v):
    return (v * 2731) >> 16


def by6(v):
    return (v * 10923) >> 16


def kernel(
    hid, wt, ids, loss_out, wg_out, hg_out,
    id_v, w_v, h_v, hp, ht_v, acc, qf, qd, cbuf, fbuf, rx, pr, lg, sg, s1, hgs, xr, zs, zr,
    sc, xst, zst, zls, lb, perm, spread,
    load_sem, a_send, a_recv, sc_send, sc_recv, st_send, st_recv, zst_send, zst_recv, zls_send, zls_recv,
    l_send, l_recv, g_send, g_recv, x_send, x_recv, z_send, z_recv,
):
    c = lax.axis_index("rep")
    v = lax.axis_index("vocab")
    y = lax.axis_index("tok")
    z, x = v // NX, v % NX
    pc = 1 - c
    R, L, O = (y + 1) % NY, (y + 3) % NY, (y + 2) % NY
    mine = y + 4 * c
    cores = (c, pc)

    def xid(d):
        return {"vocab": z * NX + (x + d) % NX}

    def zid(zz):
        return {"vocab": zz * NX + x}

    def yid(core, yy):
        return {"rep": core, "tok": yy}

    loads = [
        pltpu.make_async_copy(hid.at[0], h_v, load_sem.at[0]),
        pltpu.make_async_copy(wt.at[0, :, pl.ds(0, HALF)], w_v.at[0], load_sem.at[1]),
        pltpu.make_async_copy(wt.at[0, :, pl.ds(HALF, HALF)], w_v.at[1], load_sem.at[2]),
        pltpu.make_async_copy(ids, id_v, load_sem.at[3]),
    ]
    for cp in loads:
        cp.start()

    barrier = pltpu.get_barrier_semaphore()
    peers = [yid(cores[s], yy) for s in range(2) for yy in (y, R, L, O)][1:]
    peers += [xid(d) for d in range(1, NX)] + [zid((z + d) % NZ) for d in range(1, NZ)]
    for p in peers:
        pl.semaphore_signal(barrier, inc=1, device_id=p, device_id_type=MESH)

    def remote(src, dst, ss, rs, dev):
        return pltpu.make_async_remote_copy(
            src_ref=src, dst_ref=dst, send_sem=ss, recv_sem=rs, device_id=dev, device_id_type=MESH
        )

    sends = []

    def start(cp):
        cp.start()
        sends.append(cp)

    lane, tok = iota((ROWS, 128), 1), iota((ROWS, 128), 0)

    def to_row(cols):
        return sum(jnp.sum(jnp.where(lane == tok + 64 * i, cols[i], 0.0), axis=0, keepdims=True) for i in range(2))

    def to_col(row, i):
        return jnp.sum(jnp.where(lane == tok + 64 * i, row, 0.0), axis=1, keepdims=True)

    loads[0].wait()
    hf = h_v[...].astype(F32)
    hp[...] = jnp.concatenate(
        [hf[24 * (m + 8 * q):24 * (m + 8 * q) + 24] for m in range(CHUNKS) for q in range(2)], axis=0
    ).astype(BF16)
    for a in range(2):
        loads[1 + a].wait()
        acc[a] = dot(hp[...], w_v[a], 1, 0)
    top = jnp.maximum(
        jnp.max(jnp.abs(acc[0]), axis=1, keepdims=True), jnp.max(jnp.abs(acc[1]), axis=1, keepdims=True)
    )
    step = jnp.maximum(top, 1e-30) * (1.0 / 32767.0)
    sc[6] = jnp.concatenate(
        [to_row([step[ROWS * (b + 4 * h):ROWS * (b + 4 * h) + ROWS] for h in range(2)]) for b in range(NY)]
        + [jnp.zeros((4, 128), F32)], axis=0,
    )

    def step_of(slot, b, h):
        return to_col(sc[slot, pl.ds(b, 1)], h)

    def coded(value, by):
        return jnp.round(value * (1.0 / by)).astype(I32).astype(I16)

    def decoded(code):
        return code.astype(I32).astype(F32)

    pl.semaphore_wait(barrier, len(peers))
    for j, yy in enumerate((R, L, O)):
        for s in range(2):
            start(remote(sc.at[6], sc.at[3 * s + j], sc_send.at[3 * s + j], sc_recv.at[3 * s + j], yid(cores[s], yy)))
    for kind in range(2):
        for s in range(2):
            for a in range(2):
                near, far = ((R, L), (L, R))[a]
                i = 4 * kind + 2 * a + s
                b = (O, far)[kind]
                code = coded(acc[a, rows_of(b + 4 * cores[s])], step_of(6, b, cores[s]))
                if kind == 0:
                    qf[a, s] = code
                    start(remote(qf.at[a, s], fbuf.at[a, s], a_send.at[i], a_recv.at[i], yid(c, near)))
                else:
                    qd[a, s] = code
                    start(remote(qd.at[a, s], rx.at[0, a, s], a_send.at[i], a_recv.at[i], yid(cores[s], far)))
    for a in range(2):
        start(remote(acc.at[a, rows_of(y + 4 * pc)], pr.at[a], a_send.at[12 + a], a_recv.at[12 + a], yid(pc, y)))

    def got_step(slot):
        remote(sc.at[6], sc.at[slot], sc_send.at[slot], sc_recv.at[slot], yid(pc, y)).wait_recv()

    got_step(0)
    got_step(1)
    for s in range(2):
        for a in range(2):
            i = 2 * a + s
            near = (R, L)[a]
            remote(qf.at[a, s], fbuf.at[a, s], a_send.at[i], a_recv.at[i], yid(c, near)).wait_recv()
            by = step_of(a, near, cores[s])
            value = acc[a, rows_of(near + 4 * cores[s])] + decoded(fbuf[a, s]) * by
            cbuf[a, s] = coded(value, by + step_of(6, near, cores[s]))
            start(remote(cbuf.at[a, s], rx.at[1, a, s], a_send.at[8 + i], a_recv.at[8 + i], yid(cores[s], near)))

    ht_v[...] = hp[...].T
    loads[3].wait()
    t0 = iota((ROWS, 384), 0)
    token = mine * 24 + t0 + jnp.where(t0 >= 24, 168, 0)
    id_col = jnp.sum(jnp.where(iota((ROWS, 384), 1) == token, id_v[...][None, :], 0), axis=1, keepdims=True)
    id_col = id_col - v * (2 * HALF)
    r, t = iota((96, 96), 0), iota((96, 96), 1)
    w = r - by24(r) * 24
    perm[...] = jnp.where(t == by6(w) * 24 + by24(r) * 6 + w - by6(w) * 6, 1.0, 0.0).astype(BF16)
    r, t = iota((64, ROWS), 0), iota((64, ROWS), 1)
    inner = r & 7
    spread[...] = jnp.where((t == ((r >> 3) & 1) * 24 + (r >> 4) * 6 + inner) & (inner < 6), 1.0, 0.0).astype(BF16)

    for a in range(2):
        remote(acc.at[a, rows_of(mine)], pr.at[a], a_send.at[12 + a], a_recv.at[12 + a], yid(pc, y)).wait_recv()
    for slot in range(2, 6):
        got_step(slot)
    for s in range(2):
        steps = [step_of(3 * s + j, y, c) for j in range(3)]
        for a in range(2):
            for k in range(2):
                i = 4 + 4 * k + 2 * a + s
                remote(cbuf.at[a, s], rx.at[k, a, s], a_send.at[i], a_recv.at[i], yid(c, R)).wait_recv()
            own = acc[a, rows_of(mine)] if s == 0 else pr[a]
            lg[s, a] = own + decoded(rx[0, a, s]) * steps[1 - a] + decoded(rx[1, a, s]) * (steps[a] + steps[2])

    cols = iota((ROWS, HALF), 1)
    stats = []
    for s in range(2):
        la, lbh = lg[s, 0], lg[s, 1]
        peak = jnp.maximum(jnp.max(la, axis=1, keepdims=True), jnp.max(lbh, axis=1, keepdims=True))
        tot = [0.0] * 4
        for a, l in ((0, la), (1, lbh)):
            e = jnp.exp((l - peak) * 0.5)
            hit = cols == id_col - a * HALF
            for n, term in enumerate((e * e, e, jnp.where(hit, l, 0.0), e * (0.5 * (l - lg[1 - s, a])))):
                tot[n] = tot[n] + jnp.sum(term, axis=1, keepdims=True)
        stats.append([peak] + tot)
    xst[0] = jnp.concatenate([to_row([stats[s][n] for s in range(2)]) for n in range(5)] + [jnp.zeros((3, 128), F32)], axis=0)
    for d in range(1, NX):
        start(remote(xst.at[0], xst.at[d], st_send.at[d], st_recv.at[d], xid(d)))
    for d in range(1, NX):
        remote(xst.at[0], xst.at[d], st_send.at[d], st_recv.at[d], xid(d)).wait_recv()

    def merge(parts):
        tops = functools.reduce(jnp.maximum, [p[0:1] for p in parts])
        fs = [jnp.exp((p[0:1] - tops) * 0.5) for p in parts]
        return tops, fs, [sum(p[n:n + 1] * f for p, f in zip(parts, ws)) for n, ws in ((1, [f * f for f in fs]), (2, fs))]

    parts = [xst[d] for d in range(NX)]
    tops, fs, (norm, tau) = merge(parts)
    zst[0] = jnp.concatenate([tops, norm, tau, jnp.zeros((1, 128), F32)], axis=0)
    for d in range(1, NZ):
        start(remote(zst.at[0], zst.at[d], zst_send.at[d], zst_recv.at[d], zid((z + d) % NZ)))
    picked = sum(p[3:4] for p in parts)
    apart = sum(p[4:5] * f for p, f in zip(parts, fs))
    zls[0] = jnp.concatenate([picked, apart, jnp.zeros((2, 128), F32)], axis=0)
    for d in range(1, NZ):
        remote(zst.at[0], zst.at[d], zst_send.at[d], zst_recv.at[d], zid((z + d) % NZ)).wait_recv()
    tops, fs, (norm, tau) = merge([zst[d] for d in range(NZ)])
    log_total = tops + jnp.log(norm)
    tau_total = tops * 0.5 + jnp.log(tau)

    mr = rows_of(mine)
    log_col = [to_col(log_total, s) for s in range(2)]
    tau_col = [to_col(tau_total, s) for s in range(2)]

    def grad_copy(s, a, side):
        i = 4 * side + 2 * a + s
        src = sg.at[a, mr] if s == 0 else s1.at[a]
        return remote(src, sg.at[a, mr], g_send.at[i], g_recv.at[i], yid(cores[s], ((R, L), (L, R))[side][a]))

    for a in range(2):
        hit = jnp.where(cols == id_col - a * HALF, 1.0, 0.0)
        l = [lg[0, a], lg[1, a]]
        q = [jnp.exp(l[s] * 0.5 - tau_col[s]) for s in range(2)]
        for s in range(2):
            g = (jnp.exp(l[s] - log_col[s]) - hit + (q[s] - q[1 - s])).astype(BF16)
            if s == 0:
                sg[a, mr] = g
            else:
                s1[a] = g
        start(grad_copy(0, a, 0))
    for a in range(2):
        start(remote(s1.at[a], sg.at[a, mr], g_send.at[12 + a], g_recv.at[12 + a], yid(pc, y)))
        start(grad_copy(0, a, 1))
    for side in range(2):
        for a in range(2):
            start(grad_copy(1, a, side))
    for d in range(1, NZ):
        start(remote(zls.at[0], zls.at[d], zls_send.at[d], zls_recv.at[d], zid((z + d) % NZ)))

    pairs = [(mine, y + 4 * pc)] + [(L + 4 * cores[s], R + 4 * cores[s]) for s in range(2)] + [(O + 4 * c, O + 4 * pc)]

    def hidden_part(k):
        part = sum(
            dot(jnp.concatenate([sg[a, rows_of(m)] for m in pairs[k]], axis=0), w_v[a], 1, 1) for a in range(2)
        )
        part = dot(perm[...], part.astype(BF16), 1, 0)
        for n in range(NX):
            p = part[24 * n:24 * n + 24]
            hgs[k, n] = jnp.concatenate([p[:, :384], p[:, 384:]], axis=0).astype(BF16)
        for d in (2, 1, 3):
            start(remote(hgs.at[k, (x + d) % NX], xr.at[k, d], x_send.at[k, d], x_recv.at[k, d], xid(d)))

    def x_sum(k):
        total = hgs[k, x].astype(F32)
        for d in range(1, NX):
            remote(hgs.at[k, 0], xr.at[k, d], x_send.at[k, d], x_recv.at[k, d], xid(d)).wait_recv()
            total = total + xr[k, d].astype(F32)
        zs[k] = dot(spread[...], total.astype(BF16), 1, 0).astype(BF16)
        for g in range(4):
            zz = pairs[k][g // 2] + 8 * (g % 2)
            d = (zz - z + NZ) % NZ

            @pl.when(d != 0)
            def _():
                remote(zs.at[k, pl.ds(16 * g, 16)], zr.at[d], z_send.at[d], z_recv.at[d], zid(zz)).start()

            @pl.when(d == 0)
            def _():
                zr[0] = zs[k, 16 * g:16 * g + 16]

    def got(i, a, m):
        remote(sg.at[a, rows_of(m)], sg.at[a, rows_of(m)], g_send.at[i], g_recv.at[i], yid(c, L)).wait_recv()

    def forward(s):
        for a in range(2):
            m = (L, R)[a] + 4 * cores[s]
            got(2 * a + s, a, m)
            i = 8 + 2 * a + s
            start(remote(sg.at[a, rows_of(m)], sg.at[a, rows_of(m)], g_send.at[i], g_recv.at[i], yid(c, (R, L)[a])))

    def rest(s):
        for a in range(2):
            got(4 + 2 * a + s, a, (R, L)[a] + 4 * cores[s])

    for a in range(2):
        got(12 + a, a, pairs[0][1])
    hidden_part(0)
    forward(0)
    rest(0)
    hidden_part(1)
    forward(1)
    x_sum(0)
    rest(1)
    hidden_part(2)
    x_sum(1)

    for d in range(1, NZ):
        remote(zls.at[0], zls.at[d], zls_send.at[d], zls_recv.at[d], zid((z + d) % NZ)).wait_recv()
    late = [zls[d] for d in range(NZ)]
    picked = sum(p[0:1] for p in late)
    apart = sum(p[1:2] * f for p, f in zip(late, fs))
    ratio = pltpu.roll(apart / tau - tau_total, 64, 1) + tau_total
    loss = log_total - picked + 2.0 * ratio
    lb[mine] = jnp.concatenate([loss, jnp.zeros((7, 128), F32)], axis=0)
    for e in range(1, CHUNKS):
        m = (mine + e) % CHUNKS
        start(remote(lb.at[mine], lb.at[mine], l_send.at[e], l_recv.at[mine], yid(m // 4, m % 4)))

    for s in range(2):
        for a in range(2):
            got(8 + 2 * a + s, a, O + 4 * cores[s])
    hidden_part(3)
    x_sum(2)
    for a in range(2):
        wg_out[0, :, a * HALF:(a + 1) * HALF] = dot(ht_v[...], sg[a], 1, 0).astype(BF16)
        if a == 0:
            x_sum(3)

    for e in range(1, CHUNKS):
        m = (mine + e) % CHUNKS
        remote(lb.at[m], lb.at[m], l_send.at[e], l_recv.at[m], yid(pc, y)).wait_recv()
    lanes = iota((1, 128), 1)
    mixed = jnp.zeros((1, 128), F32)
    for i in range(4):
        m = (4 * y + i) % CHUNKS
        row = lb[m, 0:1]
        row = jnp.where(m // 4 == c, row, pltpu.roll(row, 64, 1))
        row = jnp.where(y // 2 == 0, row, pltpu.roll(row, 104, 1))
        if i:
            row = pltpu.roll(row, 24 * i, 1)
        mixed = jnp.where((lanes >= 24 * i) & (lanes < 24 * i + 24), row, mixed)
    loss_out[...] = mixed[:, :96]

    for d in range(1, NZ):
        remote(zr.at[d], zr.at[d], z_send.at[d], z_recv.at[d], zid(z)).wait_recv()
    total = sum(zr[d].astype(F32) for d in range(NZ))
    hg_out[0] = jnp.concatenate([total[:8], total[8:]], axis=1)[:6].astype(BF16)

    for cp in sends:
        cp.wait_send()
    for d in range(1, NZ):
        remote(zr.at[d], zr.at[d], z_send.at[d], z_recv.at[d], zid((z + d) % NZ)).wait_send()


def finish(*refs):
    copies = [pltpu.make_async_copy(refs[i], refs[3 + i], refs[6].at[i]) for i in range(3)]
    for cp in copies:
        cp.start()
    for cp in copies:
        cp.wait()


def body(hidden, head_weight, token_ids):
    dma = pltpu.SemaphoreType.DMA
    outs = pl.pallas_call(
        kernel,
        out_shape=(
            pltpu.VMEM((1, 96), F32),
            pltpu.VMEM((1, 768, 2 * HALF), BF16),
            pltpu.VMEM((1, 6, 768), BF16),
        ),
        in_specs=[pl.BlockSpec(memory_space=pl.ANY)] * 3,
        out_specs=(pl.BlockSpec(memory_space=pltpu.VMEM),) * 3,
        scratch_shapes=[
            pltpu.VMEM((384,), I32),
            pltpu.VMEM((2, 768, HALF), BF16),
            pltpu.VMEM((384, 768), BF16),
            pltpu.VMEM((384, 768), BF16),
            pltpu.VMEM((768, 384), BF16),
            pltpu.VMEM((2, 384, HALF), F32),
            pltpu.VMEM((2, 2, ROWS, HALF), I16),
            pltpu.VMEM((2, 2, ROWS, HALF), I16),
            pltpu.VMEM((2, 2, ROWS, HALF), I16),
            pltpu.VMEM((2, 2, ROWS, HALF), I16),
            pltpu.VMEM((2, 2, 2, ROWS, HALF), I16),
            pltpu.VMEM((2, ROWS, HALF), F32),
            pltpu.VMEM((2, 2, ROWS, HALF), F32),
            pltpu.VMEM((2, 384, HALF), BF16),
            pltpu.VMEM((2, ROWS, HALF), BF16),
            pltpu.VMEM((STEPS, NX, ROWS, 384), BF16),
            pltpu.VMEM((STEPS, NX, ROWS, 384), BF16),
            pltpu.VMEM((STEPS, 64, 384), BF16),
            pltpu.VMEM((NZ, 16, 384), BF16),
            pltpu.VMEM((7, 8, 128), F32),
            pltpu.VMEM((NX, 8, 128), F32),
            pltpu.VMEM((NZ, 4, 128), F32),
            pltpu.VMEM((NZ, 4, 128), F32),
            pltpu.VMEM((CHUNKS, 8, 128), F32),
            pltpu.VMEM((96, 96), BF16),
            pltpu.VMEM((64, ROWS), BF16),
            dma((4,)),
            dma((14,)), dma((14,)),
            dma((6,)), dma((6,)),
            dma((NX,)), dma((NX,)),
            dma((NZ,)), dma((NZ,)),
            dma((NZ,)), dma((NZ,)),
            dma((CHUNKS,)), dma((CHUNKS,)),
            dma((14,)), dma((14,)),
            dma((STEPS, NX)), dma((STEPS, NX)),
            dma((NZ,)), dma((NZ,)),
        ],
        compiler_params=pltpu.CompilerParams(
            collective_id=0, has_side_effects=True, vmem_limit_bytes=60 * 1024 * 1024
        ),
        cost_estimate=pl.CostEstimate(flops=2400000000, bytes_accessed=5000000, transcendentals=400000),
    )(hidden, head_weight, token_ids)
    return pl.pallas_call(
        finish,
        out_shape=tuple(jax.ShapeDtypeStruct(o.shape, o.dtype) for o in outs),
        in_specs=[pl.BlockSpec(memory_space=pltpu.VMEM)] * 3,
        out_specs=(pl.BlockSpec(memory_space=pl.ANY),) * 3,
        scratch_shapes=[dma((3,))],
        compiler_params=pltpu.CompilerParams(vmem_limit_bytes=1024 * 1024),
    )(*outs)


def solution(mesh):
    return jax.shard_map(
        body,
        mesh=mesh,
        in_specs=(P("rep", None, "tok"), P("rep", "tok", "vocab"), P()),
        out_specs=(P("rep", "tok"), P("rep", "tok", "vocab"), P("rep", "vocab", "tok")),
        check_vma=False,
    )
```

time: 81.7 us -> 63.9 us (0.78)
  Pallas kernels: 75.1 us -> 63.1 us
  local copies, waits for them, and re-layouts: 5.68 us -> 0 us
    pallas_call x1 -> x2, Pallas kernels: 75.1 us -> 63.1 us  [the longest x1 61.8 us: body(): pl.pallas_call(kernel, out_shape=(pltpu.VMEM((1, 96), F32), pltpu.VMEM((1...]
    unnamed x7 -> x0, local copies, waits for them, and re-layouts: 4.99 us -> none
where the time goes in v2:
time: 63.9 us; the launch traced here: 63.8 us
  Pallas kernels  63.1 us (99%)
  between operations  0.64 us (1%)
    pallas_call x1, Pallas kernels, body(): pl.pallas_call(kernel, out_shape=(pltpu.VMEM((1, 96), F32), pltpu.VMEM((1...  61.8 us
    pallas_call x1, Pallas kernels, body(): pl.pallas_call(finish, out_shape=tuple((jax.ShapeDtypeStruct(o.shape, o.d...  1.31 us

profile of v2, /device:TPU:16, one launch (start us, length us, event | category | flops | bytes accessed | tf_op | source)
XLA Modules:
  0.0 63.8 jit_solution(12880563419335343416)
XLA Ops:
  0.6 61.8 %shard_map.58 = (f32[1,96]{1,0:T(1,128)S(1)}, bf16[1,768,1280]{2,1,0:T(8,128)(2,1)S(1)}, bf16[1,6,768]{2,1,0:T(8,128)(2,1)S(1)}) custom-call(bf16[1,384,768]{2,1,0:T(8,128)(2,1)} %hid.1, bf16[1,768,1280]{2,1,0:T(8,128)(2,1)} %wt.1, s32[384]{0:T(512)} %ids.1), custom_call_target="tpu_custom_call" | custom-call | flops 2400000000 | bytes 5000000 | tf_op jit(solution)/shard_map/pallas_call | solution.py:366
  62.4 1.3 %shard_map.59 = (f32[1,96]{1,0:T(1,128)}, bf16[1,768,1280]{2,1,0:T(8,128)(2,1)}, bf16[1,6,768]{2,1,0:T(8,128)(2,1)}) custom-call(f32[1,96]{1,0:T(1,128)S(1)} %get-tuple-element.6.refs_0_, bf16[1,768,1280]{2,1,0:T(8,128)(2,1)S(1)} %get-tuple-element.7.refs_1_, bf16[1,6,768]{2,1,0:T(8,128)(2,1)S(1)} %get-tuple-element.8.refs_2_), custom_call_target="tpu_custom_call" | custom-call | tf_op jit(solution)/shard_map/pallas_call | solution.py:418

commit v3 on v2

v3 whole, which is shorter than its diff:
```python
import functools

import jax
import jax.numpy as jnp
from jax import lax
from jax.experimental import pallas as pl
from jax.experimental.pallas import tpu as pltpu
from jax.sharding import PartitionSpec as P

F32, BF16, I16, I32 = jnp.float32, jnp.bfloat16, jnp.int16, jnp.int32
NX, NZ, NY = 4, 16, 4
CHUNKS = 8
ROWS = 48
HALF = 640
PAIRS = 3
MESH = pl.DeviceIdType.MESH


def rows_of(m):
    return pl.ds(pl.multiple_of(m * ROWS, 16), ROWS)


def dot(a, b, ca, cb):
    return lax.dot_general(a, b, (((ca,), (cb,)), ((), ())), preferred_element_type=F32)


def iota(shape, dim):
    return lax.broadcasted_iota(I32, shape, dim)


def by24(v):
    return (v * 2731) >> 16


def by6(v):
    return (v * 10923) >> 16


def kernel(
    hid, wt, ids, loss_out, wg_out, hg_out,
    id_v, w_v, wt_v, h_v, hp, ht_v, acc, qf, qd, cbuf, fbuf, rx, pr, lg, sg, s1, hgs, xr, zs, zr,
    hgt, xrt, zst2, sc, xst, zst, zls, lb, perm, spread, perm1, spread1, ev,
    load_sem, a_send, a_recv, sc_send, sc_recv, st_sem, zst_sem, zls_sem, l_sem, g_send, g_recv, x_send, x_recv, z_sem,
):
    c = lax.axis_index("rep")
    v = lax.axis_index("vocab")
    y = lax.axis_index("tok")
    z, x = v // NX, v % NX
    pc = 1 - c
    R, L, O = (y + 1) % NY, (y + 3) % NY, (y + 2) % NY
    mine = y + 4 * c
    cores = (c, pc)

    def xid(d):
        return {"vocab": z * NX + (x + d) % NX}

    def zid(zz):
        return {"vocab": zz * NX + x}

    def yid(core, yy):
        return {"rep": core, "tok": yy}

    loads = [
        pltpu.make_async_copy(hid.at[0], h_v, load_sem.at[0]),
        pltpu.make_async_copy(wt.at[0, :, pl.ds(0, HALF)], w_v.at[0], load_sem.at[1]),
        pltpu.make_async_copy(wt.at[0, :, pl.ds(HALF, HALF)], w_v.at[1], load_sem.at[2]),
        pltpu.make_async_copy(ids, id_v, load_sem.at[3]),
    ]
    for cp in loads:
        cp.start()

    barrier = pltpu.get_barrier_semaphore()
    peers = [yid(cores[s], yy) for s in range(2) for yy in (y, R, L, O)][1:]
    peers += [xid(d) for d in range(1, NX)] + [zid((z + d) % NZ) for d in range(1, NZ)]
    for p in peers:
        pl.semaphore_signal(barrier, inc=1, device_id=p, device_id_type=MESH)

    def remote(src, dst, ss, rs, dev):
        return pltpu.make_async_remote_copy(
            src_ref=src, dst_ref=dst, send_sem=ss, recv_sem=rs, device_id=dev, device_id_type=MESH
        )

    def start(*copy):
        remote(*copy).start()

    def wait_in(ref, sem):
        remote(ref, ref, sem, sem, yid(pc, y)).wait_recv()

    def wait_out(ref, sem):
        remote(ref, ref, sem, sem, yid(pc, y)).wait_send()

    lane, tok = iota((ROWS, 128), 1), iota((ROWS, 128), 0)

    def to_row(cols, where=(0, 1)):
        return sum(
            jnp.sum(jnp.where(lane == tok + 64 * where[i], cols[i], 0.0), axis=0, keepdims=True) for i in range(2)
        )

    def to_col(row, i):
        return jnp.sum(jnp.where(lane == tok + 64 * i, row, 0.0), axis=1, keepdims=True)

    loads[0].wait()
    hf = h_v[...].astype(F32)
    hp[...] = jnp.concatenate(
        [hf[24 * (m + 8 * q):24 * (m + 8 * q) + 24] for m in range(CHUNKS) for q in range(2)], axis=0
    ).astype(BF16)
    for a in range(2):
        loads[1 + a].wait()

    def step_of(slot, b, h):
        return to_col(sc[slot, pl.ds(b, 1)], h)

    def coded(value, by):
        return jnp.round(value * (1.0 / by)).astype(I32).astype(I16)

    def decoded(code):
        return code.astype(I32).astype(F32)

    sc[6] = jnp.zeros((8, 128), F32)
    own = {}
    place = {"R": R, "L": L, "O": O, "y": y}

    def logits(owners):
        chunks = [(name, s) for name in owners for s in range(2)]
        ms = [rows_of(place[name] + 4 * cores[s]) for name, s in chunks]
        lhs = jnp.concatenate([hp[m] for m in ms], axis=0)
        parts = [dot(lhs, w_v[a], 1, 0) for a in range(2)]
        top = jnp.maximum(*[jnp.max(jnp.abs(p), axis=1, keepdims=True) for p in parts])
        step = jnp.maximum(top, 1e-30) * (1.0 / 32767.0)
        for n, m in enumerate(ms):
            here = slice(ROWS * n, ROWS * n + ROWS)
            for a in range(2):
                acc[a, m] = parts[a][here]
            own[chunks[n]] = step[here]
        for name in owners:
            sc[6, pl.ds(place[name], 1)] = to_row([own[name, s] for s in range(2)], cores)

    def send_coded(kind):
        for s in range(2):
            for a in range(2):
                near, far = ((R, L), (L, R))[a]
                name = ("O", "LR"[a])[kind]
                code = coded(acc[a, rows_of(place[name] + 4 * cores[s])], own[name, s])
                if kind == 0:
                    qf[a, s] = code
                    start(qf.at[a, s], fbuf.at[s, a], a_send.at[0], a_recv.at[s], yid(c, near))
                else:
                    qd[a, s] = code
                    start(qd.at[a, s], rx.at[s, 0, a], a_send.at[1], a_recv.at[2 + s], yid(cores[s], far))

    logits("O")
    pl.semaphore_wait(barrier, len(peers))
    send_coded(0)
    logits("RLy")
    for j, yy in enumerate((R, L, O)):
        for s in range(2):
            late = 1 if s or j == 2 else 0
            start(sc.at[6], sc.at[(0, 1, 4, 2, 3, 5)[3 * s + j]], sc_send.at[0], sc_recv.at[late], yid(cores[s], yy))
    slot = lambda s, j: (0, 1, 4, 2, 3, 5)[3 * s + j]
    send_coded(1)
    for a in range(2):
        start(acc.at[a, rows_of(y + 4 * pc)], pr.at[a], a_send.at[3], a_recv.at[4], yid(pc, y))

    for a in range(2):
        wt_v[a] = w_v[a].T

    wait_in(sc.at[pl.ds(0, 2)], sc_recv.at[0])
    for s in range(2):
        wait_in(fbuf.at[s], a_recv.at[s])
        for a in range(2):
            near = (R, L)[a]
            by = step_of(slot(0, a), near, cores[s])
            value = acc[a, rows_of(near + 4 * cores[s])] + decoded(fbuf[s, a]) * by
            cbuf[a, s] = coded(value, by + own["RL"[a], s])
            start(cbuf.at[a, s], rx.at[s, 1, a], a_send.at[2], a_recv.at[2 + s], yid(cores[s], near))

    ht_v[...] = hp[...].T
    loads[3].wait()
    t0 = iota((ROWS, 384), 0)
    token = mine * 24 + t0 + jnp.where(t0 >= 24, 168, 0)
    id_col = jnp.sum(jnp.where(iota((ROWS, 384), 1) == token, id_v[...][None, :], 0), axis=1, keepdims=True)
    id_col = id_col - v * (2 * HALF)
    r, t = iota((96, 96), 0), iota((96, 96), 1)
    w = r - by24(r) * 24
    perm[...] = jnp.where(t == by6(w) * 24 + by24(r) * 6 + w - by6(w) * 6, 1.0, 0.0).astype(BF16)
    r, t = iota((64, ROWS), 0), iota((64, ROWS), 1)
    inner = r & 7
    spread[...] = jnp.where((t == ((r >> 3) & 1) * 24 + (r >> 4) * 6 + inner) & (inner < 6), 1.0, 0.0).astype(BF16)

    r, t = iota((64, ROWS), 0), iota((64, ROWS), 1)
    w = r & 15
    perm1[...] = jnp.where((t == by6(w) * 24 + (r >> 4) * 6 + w - by6(w) * 6) & (w < 12), 1.0, 0.0).astype(BF16)
    r, t = iota((32, 32), 0), iota((32, 32), 1)
    inner = r & 7
    spread1[...] = jnp.where((t == ((r >> 3) & 1) * 16 + (r >> 4) * 6 + inner) & (inner < 6), 1.0, 0.0).astype(BF16)

    wait_in(pr, a_recv.at[4])
    wait_in(sc.at[pl.ds(2, 4)], sc_recv.at[1])
    cols = iota((ROWS, HALF), 1)
    stats = []
    for s in range(2):
        steps = [step_of(slot(s, j), y, c) for j in range(3)]
        wait_in(rx.at[s], a_recv.at[2 + s])
        for a in range(2):
            base = acc[a, rows_of(mine)] if s == 0 else pr[a]
            lg[s, a] = base + decoded(rx[s, 0, a]) * steps[1 - a] + decoded(rx[s, 1, a]) * (steps[a] + steps[2])
        peak = jnp.maximum(*[jnp.max(lg[s, a], axis=1, keepdims=True) for a in range(2)])
        tot = [0.0] * 3
        for a in range(2):
            l = lg[s, a]
            e = jnp.exp((l - peak) * 0.5)
            ev[s, a] = e
            hit = cols == id_col - a * HALF
            for n, term in enumerate((e * e, e, jnp.where(hit, l, 0.0))):
                tot[n] = tot[n] + jnp.sum(term, axis=1, keepdims=True)
        stats.append([peak] + tot)
    for s in range(2):
        stats[s].append(sum(
            jnp.sum(ev[s, a] * (0.5 * (lg[s, a] - lg[1 - s, a])), axis=1, keepdims=True) for a in range(2)
        ))
    xst[0] = jnp.concatenate([to_row([stats[s][n] for s in range(2)]) for n in range(5)] + [jnp.zeros((3, 128), F32)], axis=0)
    for d in range(1, NX):
        start(xst.at[0], xst.at[d], st_sem.at[0], st_sem.at[1], xid(d))
    wait_in(xst.at[pl.ds(1, NX - 1)], st_sem.at[1])

    def merge(parts):
        tops = functools.reduce(jnp.maximum, [p[0:1] for p in parts])
        fs = [jnp.exp((p[0:1] - tops) * 0.5) for p in parts]
        return tops, fs, [sum(p[n:n + 1] * f for p, f in zip(parts, ws)) for n, ws in ((1, [f * f for f in fs]), (2, fs))]

    parts = [xst[d] for d in range(NX)]
    tops, fs, (norm, tau) = merge(parts)
    zst[0] = jnp.concatenate([tops, norm, tau, jnp.zeros((1, 128), F32)], axis=0)
    for d in range(1, NZ):
        start(zst.at[0], zst.at[d], zst_sem.at[0], zst_sem.at[1], zid((z + d) % NZ))
    picked = sum(p[3:4] for p in parts)
    apart = sum(p[4:5] * f for p, f in zip(parts, fs))
    zls[0] = jnp.concatenate([picked, apart, jnp.zeros((2, 128), F32)], axis=0)
    wait_in(zst.at[pl.ds(1, NZ - 1)], zst_sem.at[1])
    tops, fs, (norm, tau) = merge([zst[d] for d in range(NZ)])
    log_total = tops + jnp.log(norm)
    tau_total = tops * 0.5 + jnp.log(tau)

    mr = rows_of(mine)
    log_col = [to_col(log_total, s) for s in range(2)]
    tau_col = [to_col(tau_total, s) for s in range(2)]

    def send_grad(s, a, side):
        src = sg.at[a, mr] if s == 0 else s1.at[a]
        start(src, sg.at[a, mr], g_send.at[1 - s], g_recv.at[2 * side + s], yid(cores[s], ((R, L), (L, R))[side][a]))

    for a in range(2):
        hit = jnp.where(cols == id_col - a * HALF, 1.0, 0.0)
        l = [lg[0, a], lg[1, a]]
        q = [jnp.exp(l[s] * 0.5 - tau_col[s]) for s in range(2)]
        for s in range(2):
            g = (jnp.exp(l[s] - log_col[s]) - hit + (q[s] - q[1 - s])).astype(BF16)
            if s == 0:
                sg[a, mr] = g
            else:
                s1[a] = g
        send_grad(0, a, 0)
    for a in range(2):
        start(s1.at[a], sg.at[a, mr], g_send.at[0], g_recv.at[4], yid(pc, y))
        send_grad(0, a, 1)
    for d in range(1, NZ):
        start(zls.at[0], zls.at[d], zls_sem.at[0], zls_sem.at[1], zid((z + d) % NZ))

    steps = [(mine, y + 4 * pc)] + [(L + 4 * cores[s], R + 4 * cores[s]) for s in range(2)]
    steps += [(O + 4 * cores[s],) for s in range(2)]

    def buffers(k):
        return (hgs, xr, zs, perm, spread, k, ROWS) if k < PAIRS else (hgt, xrt, zst2, perm1, spread1, k - PAIRS, 32)

    def hidden_part(k):
        hg, xb, _, order, _, n, rows = buffers(k)
        part = sum(
            dot(jnp.concatenate([sg[a, rows_of(m)] for m in steps[k]], axis=0), wt_v[a], 1, 0) for a in range(2)
        )
        part = dot(order[...], part.astype(BF16), 1, 0)
        for q in range(NX):
            p = part[rows // 2 * q:rows // 2 * q + rows // 2]
            hg[n, q] = jnp.concatenate([p[:, :384], p[:, 384:]], axis=0).astype(BF16)
        for d in (2, 1, 3):
            start(hg.at[n, (x + d) % NX], xb.at[n, d], x_send.at[k // PAIRS], x_recv.at[k], xid(d))

    def x_sum(k):
        hg, xb, zb, _, order, n, rows = buffers(k)
        wait_in(xb.at[n, pl.ds(1, NX - 1)], x_recv.at[k])
        total = hg[n, x].astype(F32)
        for d in range(1, NX):
            total = total + xb[n, d].astype(F32)
        zb[n] = dot(order[...], total.astype(BF16), 1, 0).astype(BF16)
        for g in range(2 * len(steps[k])):
            zz = steps[k][g // 2] + 8 * (g % 2)
            d = (zz - z + NZ) % NZ

            @pl.when(d != 0)
            def _():
                start(zb.at[n, pl.ds(16 * g, 16)], zr.at[d], z_sem.at[0], z_sem.at[1], zid(zz))

            @pl.when(d == 0)
            def _():
                zr[0] = zb[n, 16 * g:16 * g + 16]

    def two(m):
        return sg.at[:, rows_of(m)]

    def forward(s):
        wait_in(two(L + 4 * cores[s]), g_recv.at[s])
        for a in range(2):
            m = rows_of((L, R)[a] + 4 * cores[s])
            start(sg.at[a, m], sg.at[a, m], g_send.at[0], g_recv.at[5 + s], yid(c, (R, L)[a]))

    wait_in(two(y + 4 * pc), g_recv.at[4])
    hidden_part(0)
    wait_out(sg.at[:, pl.ds(0, 2 * ROWS)], g_send.at[1])
    for side in range(2):
        for a in range(2):
            send_grad(1, a, side)
    for s in range(2):
        forward(s)
        wait_in(two(L + 4 * cores[s]), g_recv.at[2 + s])
        hidden_part(1 + s)
        x_sum(s)

    wait_in(zls.at[pl.ds(1, NZ - 1)], zls_sem.at[1])
    late = [zls[d] for d in range(NZ)]
    picked = sum(p[0:1] for p in late)
    apart = sum(p[1:2] * f for p, f in zip(late, fs))
    ratio = pltpu.roll(apart / tau - tau_total, 64, 1) + tau_total
    loss = log_total - picked + 2.0 * ratio
    lb[0] = jnp.concatenate([loss, jnp.zeros((7, 128), F32)], axis=0)
    for e in range(1, CHUNKS):
        m = (mine + e) % CHUNKS
        start(lb.at[0], lb.at[e], l_sem.at[0], l_sem.at[1], yid(m // 4, m % 4))
    for s in range(2):
        wait_in(two(O + 4 * cores[s]), g_recv.at[5 + s])
        hidden_part(3 + s)
    x_sum(2)
    for a in range(2):
        wg_out[0, :, a * HALF:(a + 1) * HALF] = dot(ht_v[...], sg[a], 1, 0).astype(BF16)
        x_sum(3 + a)

    wait_in(lb.at[pl.ds(1, CHUNKS - 1)], l_sem.at[1])
    lanes = iota((1, 128), 1)
    mixed = jnp.zeros((1, 128), F32)
    for i in range(4):
        m = (4 * y + i) % CHUNKS
        row = lb[(mine - m + CHUNKS) % CHUNKS, 0:1]
        row = jnp.where(m // 4 == c, row, pltpu.roll(row, 64, 1))
        row = jnp.where(y // 2 == 0, row, pltpu.roll(row, 104, 1))
        if i:
            row = pltpu.roll(row, 24 * i, 1)
        mixed = jnp.where((lanes >= 24 * i) & (lanes < 24 * i + 24), row, mixed)
    loss_out[...] = mixed[:, :96]

    wait_in(zr.at[pl.ds(1, NZ - 1)], z_sem.at[1])
    total = sum(zr[d].astype(F32) for d in range(NZ))
    hg_out[0] = jnp.concatenate([total[:8], total[8:]], axis=1)[:6].astype(BF16)

    wait_out(qf, a_send.at[0])
    wait_out(qd, a_send.at[1])
    wait_out(cbuf, a_send.at[2])
    wait_out(pr, a_send.at[3])
    wait_out(sc.at[pl.ds(0, 6)], sc_send.at[0])
    wait_out(xst.at[pl.ds(1, NX - 1)], st_sem.at[0])
    wait_out(zst.at[pl.ds(1, NZ - 1)], zst_sem.at[0])
    wait_out(zls.at[pl.ds(1, NZ - 1)], zls_sem.at[0])
    wait_out(lb.at[pl.ds(1, CHUNKS - 1)], l_sem.at[0])
    wait_out(sg.at[:, pl.ds(0, 5 * ROWS)], g_send.at[0])
    wait_out(xr.at[:, pl.ds(1, NX - 1)], x_send.at[0])
    wait_out(xrt.at[:, pl.ds(1, NX - 1)], x_send.at[1])
    wait_out(zr.at[pl.ds(1, NZ - 1)], z_sem.at[0])


def finish(*refs):
    copies = [pltpu.make_async_copy(refs[i], refs[3 + i], refs[6].at[i]) for i in range(3)]
    for cp in copies:
        cp.start()
    for cp in copies:
        cp.wait()


def body(hidden, head_weight, token_ids):
    dma = pltpu.SemaphoreType.DMA
    outs = pl.pallas_call(
        kernel,
        out_shape=(
            pltpu.VMEM((1, 96), F32),
            pltpu.VMEM((1, 768, 2 * HALF), BF16),
            pltpu.VMEM((1, 6, 768), BF16),
        ),
        in_specs=[pl.BlockSpec(memory_space=pl.ANY)] * 3,
        out_specs=(pl.BlockSpec(memory_space=pltpu.VMEM),) * 3,
        scratch_shapes=[
            pltpu.VMEM((384,), I32),
            pltpu.VMEM((2, 768, HALF), BF16),
            pltpu.VMEM((2, HALF, 768), BF16),
            pltpu.VMEM((384, 768), BF16),
            pltpu.VMEM((384, 768), BF16),
            pltpu.VMEM((768, 384), BF16),
            pltpu.VMEM((2, 384, HALF), F32),
            pltpu.VMEM((2, 2, ROWS, HALF), I16),
            pltpu.VMEM((2, 2, ROWS, HALF), I16),
            pltpu.VMEM((2, 2, ROWS, HALF), I16),
            pltpu.VMEM((2, 2, ROWS, HALF), I16),
            pltpu.VMEM((2, 2, 2, ROWS, HALF), I16),
            pltpu.VMEM((2, ROWS, HALF), F32),
            pltpu.VMEM((2, 2, ROWS, HALF), F32),
            pltpu.VMEM((2, 384, HALF), BF16),
            pltpu.VMEM((2, ROWS, HALF), BF16),
            pltpu.VMEM((PAIRS, NX, ROWS, 384), BF16),
            pltpu.VMEM((PAIRS, NX, ROWS, 384), BF16),
            pltpu.VMEM((PAIRS, 64, 384), BF16),
            pltpu.VMEM((NZ, 16, 384), BF16),
            pltpu.VMEM((2, NX, 32, 384), BF16),
            pltpu.VMEM((2, NX, 32, 384), BF16),
            pltpu.VMEM((2, 32, 384), BF16),
            pltpu.VMEM((7, 8, 128), F32),
            pltpu.VMEM((NX, 8, 128), F32),
            pltpu.VMEM((NZ, 4, 128), F32),
            pltpu.VMEM((NZ, 4, 128), F32),
            pltpu.VMEM((CHUNKS, 8, 128), F32),
            pltpu.VMEM((96, 96), BF16),
            pltpu.VMEM((64, ROWS), BF16),
            pltpu.VMEM((64, ROWS), BF16),
            pltpu.VMEM((32, 32), BF16),
            pltpu.VMEM((2, 2, ROWS, HALF), F32),
            dma((4,)),
            dma((4,)), dma((5,)),
            dma((1,)), dma((2,)),
            dma((2,)), dma((2,)), dma((2,)), dma((2,)),
            dma((2,)), dma((7,)),
            dma((2,)), dma((PAIRS + 2,)),
            dma((2,)),
        ],
        compiler_params=pltpu.CompilerParams(
            collective_id=0, has_side_effects=True, vmem_limit_bytes=60 * 1024 * 1024
        ),
        cost_estimate=pl.CostEstimate(flops=2400000000, bytes_accessed=5000000, transcendentals=400000),
    )(hidden, head_weight, token_ids)
    return pl.pallas_call(
        finish,
        out_shape=tuple(jax.ShapeDtypeStruct(o.shape, o.dtype) for o in outs),
        in_specs=[pl.BlockSpec(memory_space=pltpu.VMEM)] * 3,
        out_specs=(pl.BlockSpec(memory_space=pl.ANY),) * 3,
        scratch_shapes=[dma((3,))],
        compiler_params=pltpu.CompilerParams(vmem_limit_bytes=1024 * 1024),
    )(*outs)


def solution(mesh):
    return jax.shard_map(
        body,
        mesh=mesh,
        in_specs=(P("rep", None, "tok"), P("rep", "tok", "vocab"), P()),
        out_specs=(P("rep", "tok"), P("rep", "tok", "vocab"), P("rep", "vocab", "tok")),
        check_vma=False,
    )
```

time: 63.9 us -> 61 us (0.955)
  Pallas kernels: 63.1 us -> 60.2 us
    pallas_call x1, Pallas kernels: 61.8 us -> 58.9 us  [body(): pl.pallas_call(kernel, out_shape=(pltpu.VMEM((1, 96), F32), pltpu.VMEM((1...]
where the time goes in v3:
time: 61 us; the launch traced here: 60.8 us
  Pallas kernels  60.2 us (99%)
  between operations  0.64 us (1%)
    pallas_call x1, Pallas kernels, body(): pl.pallas_call(kernel, out_shape=(pltpu.VMEM((1, 96), F32), pltpu.VMEM((1...  58.9 us
    pallas_call x1, Pallas kernels, body(): pl.pallas_call(finish, out_shape=tuple((jax.ShapeDtypeStruct(o.shape, o.d...  1.31 us

profile of v3, /device:TPU:16, one launch (start us, length us, event | category | flops | bytes accessed | tf_op | source)
XLA Modules:
  0.0 60.8 jit_solution(16211291609695490318)
XLA Ops:
  0.6 58.9 %shard_map.58 = (f32[1,96]{1,0:T(1,128)S(1)}, bf16[1,768,1280]{2,1,0:T(8,128)(2,1)S(1)}, bf16[1,6,768]{2,1,0:T(8,128)(2,1)S(1)}) custom-call(bf16[1,384,768]{2,1,0:T(8,128)(2,1)} %hid.1, bf16[1,768,1280]{2,1,0:T(8,128)(2,1)} %wt.1, s32[384]{0:T(512)} %ids.1), custom_call_target="tpu_custom_call" | custom-call | flops 2400000000 | bytes 5000000 | tf_op jit(solution)/shard_map/pallas_call | solution.py:387
  59.5 1.3 %shard_map.59 = (f32[1,96]{1,0:T(1,128)}, bf16[1,768,1280]{2,1,0:T(8,128)(2,1)}, bf16[1,6,768]{2,1,0:T(8,128)(2,1)}) custom-call(f32[1,96]{1,0:T(1,128)S(1)} %get-tuple-element.6.refs_0_, bf16[1,768,1280]{2,1,0:T(8,128)(2,1)S(1)} %get-tuple-element.7.refs_1_, bf16[1,6,768]{2,1,0:T(8,128)(2,1)S(1)} %get-tuple-element.8.refs_2_), custom_call_target="tpu_custom_call" | custom-call | tf_op jit(solution)/shard_map/pallas_call | solution.py:443

commit v4 on v3

--- a/solution.py
+++ b/solution.py
@@ -39,7 +39,7 @@
 def kernel(
     hid, wt, ids, loss_out, wg_out, hg_out,
     id_v, w_v, wt_v, h_v, hp, ht_v, acc, qf, qd, cbuf, fbuf, rx, pr, lg, sg, s1, hgs, xr, zs, zr,
-    hgt, xrt, zst2, sc, xst, zst, zls, lb, perm, spread, perm1, spread1, ev,
+    hgt, xrt, zst2, sc, sce, xst, zst, zls, lb, perm, spread, perm1, spread1, ev,
     load_sem, a_send, a_recv, sc_send, sc_recv, st_sem, zst_sem, zls_sem, l_sem, g_send, g_recv, x_send, x_recv, z_sem,
 ):
     c = lax.axis_index("rep")
@@ -150,13 +150,14 @@
 
     logits("O")
     pl.semaphore_wait(barrier, len(peers))
+    sce[2] = jnp.broadcast_to(to_row([own["O", s] for s in range(2)], cores), (8, 128))
+    for a in range(2):
+        start(sce.at[2], sce.at[a], sc_send.at[1], sc_recv.at[0], yid(c, (R, L)[a]))
     send_coded(0)
     logits("RLy")
     for j, yy in enumerate((R, L, O)):
         for s in range(2):
-            late = 1 if s or j == 2 else 0
-            start(sc.at[6], sc.at[(0, 1, 4, 2, 3, 5)[3 * s + j]], sc_send.at[0], sc_recv.at[late], yid(cores[s], yy))
-    slot = lambda s, j: (0, 1, 4, 2, 3, 5)[3 * s + j]
+            start(sc.at[6], sc.at[3 * s + j], sc_send.at[0], sc_recv.at[1], yid(cores[s], yy))
     send_coded(1)
     for a in range(2):
         start(acc.at[a, rows_of(y + 4 * pc)], pr.at[a], a_send.at[3], a_recv.at[4], yid(pc, y))
@@ -164,12 +165,12 @@
     for a in range(2):
         wt_v[a] = w_v[a].T
 
-    wait_in(sc.at[pl.ds(0, 2)], sc_recv.at[0])
+    wait_in(sce.at[pl.ds(0, 2)], sc_recv.at[0])
     for s in range(2):
         wait_in(fbuf.at[s], a_recv.at[s])
         for a in range(2):
             near = (R, L)[a]
-            by = step_of(slot(0, a), near, cores[s])
+            by = to_col(sce[a, 0:1], cores[s])
             value = acc[a, rows_of(near + 4 * cores[s])] + decoded(fbuf[s, a]) * by
             cbuf[a, s] = coded(value, by + own["RL"[a], s])
             start(cbuf.at[a, s], rx.at[s, 1, a], a_send.at[2], a_recv.at[2 + s], yid(cores[s], near))
@@ -195,11 +196,11 @@
     spread1[...] = jnp.where((t == ((r >> 3) & 1) * 16 + (r >> 4) * 6 + inner) & (inner < 6), 1.0, 0.0).astype(BF16)
 
     wait_in(pr, a_recv.at[4])
-    wait_in(sc.at[pl.ds(2, 4)], sc_recv.at[1])
+    wait_in(sc.at[pl.ds(0, 6)], sc_recv.at[1])
     cols = iota((ROWS, HALF), 1)
     stats = []
     for s in range(2):
-        steps = [step_of(slot(s, j), y, c) for j in range(3)]
+        steps = [step_of(3 * s + j, y, c) for j in range(3)]
         wait_in(rx.at[s], a_recv.at[2 + s])
         for a in range(2):
             base = acc[a, rows_of(mine)] if s == 0 else pr[a]
@@ -236,6 +237,8 @@
     picked = sum(p[3:4] for p in parts)
     apart = sum(p[4:5] * f for p, f in zip(parts, fs))
     zls[0] = jnp.concatenate([picked, apart, jnp.zeros((2, 128), F32)], axis=0)
+    for d in range(1, NZ):
+        start(zls.at[0], zls.at[d], zls_sem.at[0], zls_sem.at[1], zid((z + d) % NZ))
     wait_in(zst.at[pl.ds(1, NZ - 1)], zst_sem.at[1])
     tops, fs, (norm, tau) = merge([zst[d] for d in range(NZ)])
     log_total = tops + jnp.log(norm)
@@ -263,8 +266,6 @@
     for a in range(2):
         start(s1.at[a], sg.at[a, mr], g_send.at[0], g_recv.at[4], yid(pc, y))
         send_grad(0, a, 1)
-    for d in range(1, NZ):
-        start(zls.at[0], zls.at[d], zls_sem.at[0], zls_sem.at[1], zid((z + d) % NZ))
 
     steps = [(mine, y + 4 * pc)] + [(L + 4 * cores[s], R + 4 * cores[s]) for s in range(2)]
     steps += [(O + 4 * cores[s],) for s in range(2)]
@@ -314,15 +315,17 @@
 
     wait_in(two(y + 4 * pc), g_recv.at[4])
     hidden_part(0)
-    wait_out(sg.at[:, pl.ds(0, 2 * ROWS)], g_send.at[1])
     for side in range(2):
         for a in range(2):
             send_grad(1, a, side)
-    for s in range(2):
-        forward(s)
-        wait_in(two(L + 4 * cores[s]), g_recv.at[2 + s])
-        hidden_part(1 + s)
-        x_sum(s)
+    forward(0)
+    wait_in(two(L + 4 * c), g_recv.at[2])
+    hidden_part(1)
+    forward(1)
+    x_sum(0)
+    wait_in(two(L + 4 * pc), g_recv.at[3])
+    hidden_part(2)
+    x_sum(1)
 
     wait_in(zls.at[pl.ds(1, NZ - 1)], zls_sem.at[1])
     late = [zls[d] for d in range(NZ)]
@@ -364,11 +367,13 @@
     wait_out(cbuf, a_send.at[2])
     wait_out(pr, a_send.at[3])
     wait_out(sc.at[pl.ds(0, 6)], sc_send.at[0])
+    wait_out(sce.at[pl.ds(0, 2)], sc_send.at[1])
     wait_out(xst.at[pl.ds(1, NX - 1)], st_sem.at[0])
     wait_out(zst.at[pl.ds(1, NZ - 1)], zst_sem.at[0])
     wait_out(zls.at[pl.ds(1, NZ - 1)], zls_sem.at[0])
     wait_out(lb.at[pl.ds(1, CHUNKS - 1)], l_sem.at[0])
     wait_out(sg.at[:, pl.ds(0, 5 * ROWS)], g_send.at[0])
+    wait_out(sg.at[:, pl.ds(0, 2 * ROWS)], g_send.at[1])
     wait_out(xr.at[:, pl.ds(1, NX - 1)], x_send.at[0])
     wait_out(xrt.at[:, pl.ds(1, NX - 1)], x_send.at[1])
     wait_out(zr.at[pl.ds(1, NZ - 1)], z_sem.at[0])
@@ -418,6 +423,7 @@
             pltpu.VMEM((2, NX, 32, 384), BF16),
             pltpu.VMEM((2, 32, 384), BF16),
             pltpu.VMEM((7, 8, 128), F32),
+            pltpu.VMEM((3, 8, 128), F32),
             pltpu.VMEM((NX, 8, 128), F32),
             pltpu.VMEM((NZ, 4, 128), F32),
             pltpu.VMEM((NZ, 4, 128), F32),
@@ -429,7 +435,7 @@
             pltpu.VMEM((2, 2, ROWS, HALF), F32),
             dma((4,)),
             dma((4,)), dma((5,)),
-            dma((1,)), dma((2,)),
+            dma((2,)), dma((2,)),
             dma((2,)), dma((2,)), dma((2,)), dma((2,)),
             dma((2,)), dma((7,)),
             dma((2,)), dma((PAIRS + 2,)),

time: 61 us -> 60.9 us (level)
  no operation moved by 1% of the time
where the time goes in v4:
time: 60.9 us; the launch traced here: 60.8 us
  Pallas kernels  60.1 us (99%)
  between operations  0.64 us (1%)
    pallas_call x1, Pallas kernels, body(): pl.pallas_call(kernel, out_shape=(pltpu.VMEM((1, 96), F32), pltpu.VMEM((1...  58.8 us
    pallas_call x1, Pallas kernels, body(): pl.pallas_call(finish, out_shape=tuple((jax.ShapeDtypeStruct(o.shape, o.d...  1.31 us

profile of v4, /device:TPU:16, one launch (start us, length us, event | category | flops | bytes accessed | tf_op | source)
XLA Modules:
  0.0 60.8 jit_solution(14281420111119806327)
XLA Ops:
  0.6 58.8 %shard_map.58 = (f32[1,96]{1,0:T(1,128)S(1)}, bf16[1,768,1280]{2,1,0:T(8,128)(2,1)S(1)}, bf16[1,6,768]{2,1,0:T(8,128)(2,1)S(1)}) custom-call(bf16[1,384,768]{2,1,0:T(8,128)(2,1)} %hid.1, bf16[1,768,1280]{2,1,0:T(8,128)(2,1)} %wt.1, s32[384]{0:T(512)} %ids.1), custom_call_target="tpu_custom_call" | custom-call | flops 2400000000 | bytes 5000000 | tf_op jit(solution)/shard_map/pallas_call | solution.py:392
  59.5 1.3 %shard_map.59 = (f32[1,96]{1,0:T(1,128)}, bf16[1,768,1280]{2,1,0:T(8,128)(2,1)}, bf16[1,6,768]{2,1,0:T(8,128)(2,1)}) custom-call(f32[1,96]{1,0:T(1,128)S(1)} %get-tuple-element.6.refs_0_, bf16[1,768,1280]{2,1,0:T(8,128)(2,1)S(1)} %get-tuple-element.7.refs_1_, bf16[1,6,768]{2,1,0:T(8,128)(2,1)S(1)} %get-tuple-element.8.refs_2_), custom_call_target="tpu_custom_call" | custom-call | tf_op jit(solution)/shard_map/pallas_call | solution.py:449
